TPU v7x, 32 devices: a whole 2x2x4 slice. The times are simulated.
32 devices in a mesh: row: 4 (over y, core), col: 8 (over z, x).
Axes of the slice: x: 2, y: 2, z: 4, core: 2. Of those that a mesh axis runs over, the one named last changes fastest.
Arguments:
- orbitals: bfloat16 [64, 8, 48, 2304], P(('row', 'col')), may hold values from -6 to 6
- potential_boxes: float32 [64, 48, 2304], P(('row', 'col')), may hold values from 0 to 2
- corners: int32 [64, 3], P(('row', 'col')), may hold values from 0 to 511, as said below
- signs: int32 [64], P(('row', 'col')), may hold values from -1 to 1, as said below
- counts: int32 [64], P(('row', 'col')), may hold values from 1 to 8, as said below
Outputs:
- filtered: bfloat16 [64, 8, 48, 2304], P(('row', 'col'))
- density: float32 [64, 64, 512], P('row', 'col')
- hartree: float32 [64, 64, 512], P('row', 'col')
Inputs may be any that keep to these rules, and one draw needn't show every extreme that they name: `corners`: for fragment f held at index d = f // 2 of the row+col axis, with r = d // 8 and c = d % 8, the corner's first entry lies in [r * 16, (r + 1) * 16) and its second in [c * 8, (c + 1) * 8); the third is any cell below 512. Fragments 2 i and 2 i + 1 have the same corner. Each entry is -1 or 1; fragments 2 i and 2 i + 1 have opposite signs. Fragments 2 i and 2 i + 1 have equal counts; some device holds a fragment with 8 and some device one with 1.
All inputs are finite; a program needn't handle non-finite values.
Results may differ from a plain program's by a relative error of at most 0.001.
Values may be sent and summed in bfloat16 or wider, within the bound.
A program may use at most 128 MiB of HBM per device.

v0:
```python
import math

import jax
import jax.numpy as jnp
from jax import lax
from jax.sharding import PartitionSpec as P

B = 48
DEGREE = 6
CX = 16
CY = 8
NZ = 512


CENTER = 5.25
HALF_WIDTH = 3.75
SCREEN = 0.0025
HIGHEST = lax.Precision.HIGHEST


def passed_along(value, axis, by):
    peers = lax.axis_size(axis)
    return lax.ppermute(value, axis, [(i, (i + by) % peers) for i in range(peers)])


def hamiltonian(field, potential):
    side = field.shape[0]
    zpos = lax.broadcasted_iota(jnp.int32, field.shape, 1) % side
    zero_row = jnp.zeros_like(field[:1])
    next_x = jnp.concatenate([field[1:], zero_row], 0)
    prev_x = jnp.concatenate([zero_row, field[:-1]], 0)
    zero_col = jnp.zeros_like(field[:, :1])
    next_z = jnp.concatenate([field[:, 1:], zero_col], 1)
    prev_z = jnp.concatenate([zero_col, field[:, :-1]], 1)
    next_z = jnp.where(zpos == side - 1, 0.0, next_z)
    prev_z = jnp.where(zpos == 0, 0.0, prev_z)
    zero_plane = jnp.zeros_like(field[:, :side])
    next_y = jnp.concatenate([field[:, side:], zero_plane], 1)
    prev_y = jnp.concatenate([zero_plane, field[:, :-side]], 1)
    beside = next_x + prev_x + next_z + prev_z + next_y + prev_y
    return (3.0 + potential) * field - 0.5 * beside


def chebyshev(start, potential):

    def shifted(field):
        return (hamiltonian(field, potential) - CENTER * field) / HALF_WIDTH

    previous = start
    current = shifted(start)
    for order in range(2, DEGREE + 1):
        previous, current = (current, 2.0 * shifted(current) - previous)
    scale = lax.rsqrt(jnp.mean(current * current) + 1e-06)
    return current * scale


def filter_fragment(orbital_set, potential, live_count):

    def advance(index, carry):
        result, box_density = carry
        single = lax.dynamic_index_in_dim(orbital_set, index, 0, keepdims=False).astype(jnp.float32)
        smooth = chebyshev(single, potential)
        result = lax.dynamic_update_index_in_dim(result, smooth.astype(jnp.bfloat16), index, 0)
        return (result, box_density + smooth * smooth)

    initial = (jnp.zeros(orbital_set.shape, jnp.bfloat16), jnp.zeros(potential.shape, jnp.float32))
    return lax.fori_loop(0, live_count, advance, initial)


def place_all(slab, cubes, offsets, lift):
    start = (offsets[0, 1] + lift, offsets[0, 0], offsets[0, 2])
    slab = lax.dynamic_update_slice(slab, jnp.transpose(cubes[0], (1, 0, 2)), start)
    return slab


def wrap_depth(slab):
    head = slab[:, :, :NZ]
    return head.at[:, :, :B].add(slab[:, :, NZ:])


def wave_square(length, positions):
    signed_index = jnp.where(positions <= length // 2, positions, positions - length).astype(
        jnp.float32
    )
    wave = signed_index * (2 * math.pi / length)
    return wave * wave


def tables(length):
    product = (
        lax.broadcasted_iota(jnp.int32, (length, length), 0)
        * lax.broadcasted_iota(jnp.int32, (length, length), 1)
        % length
    )
    angle = product.astype(jnp.float32) * (2 * math.pi / length)
    return (jnp.cos(angle), jnp.sin(angle))


def along_last(real_part, imag_part, cosines, sines, sign):
    real_cos = jnp.einsum("abn,nk->abk", real_part, cosines, precision=HIGHEST)
    real_sin = jnp.einsum("abn,nk->abk", real_part, sines, precision=HIGHEST)
    imag_cos = jnp.einsum("abn,nk->abk", imag_part, cosines, precision=HIGHEST)
    imag_sin = jnp.einsum("abn,nk->abk", imag_part, sines, precision=HIGHEST)
    return (real_cos - sign * imag_sin, imag_cos + sign * real_sin)


def along_first(real_part, imag_part, cosines, sines, sign):
    real_cos = jnp.einsum("nab,nk->kab", real_part, cosines, precision=HIGHEST)
    real_sin = jnp.einsum("nab,nk->kab", real_part, sines, precision=HIGHEST)
    imag_cos = jnp.einsum("nab,nk->kab", imag_part, cosines, precision=HIGHEST)
    imag_sin = jnp.einsum("nab,nk->kab", imag_part, sines, precision=HIGHEST)
    return (real_cos - sign * imag_sin, imag_cos + sign * real_sin)


def shards(orbitals, potential_boxes, corners, signs, counts):
    frag_dev = orbitals.shape[0]
    last_slot = frag_dev - 1
    last_count = counts[last_slot]
    filtered_list = []
    density_list = []
    for fragment in range(frag_dev):
        live_count = counts[fragment] if fragment < last_slot else last_count
        result, box_density = filter_fragment(
            orbitals[fragment], potential_boxes[fragment], live_count
        )
        filtered_list.append(result)
        density_list.append(box_density)
    filtered = jnp.stack(filtered_list)
    signed = jnp.stack(density_list) * signs.astype(jnp.float32)[:, None, None]
    paired = signed[0::2] + signed[1::2]
    pair_count = frag_dev // 2
    row_start = lax.axis_index("row") * CX
    col_start = lax.axis_index("col") * CY
    offsets = jnp.stack(
        [corners[0::2, 0] - row_start, corners[0::2, 1] - col_start, corners[0::2, 2]], axis=1
    )
    reach_x = (CX + B - 2) // CX + 1
    reach_y = (CY + B - 2) // CY + 1
    slab = jnp.zeros((reach_y * CY, reach_x * CX, NZ + B), jnp.float32)
    slab = place_all(slab, paired.reshape(pair_count, B, B, B), offsets, 0)
    slab = wrap_depth(slab)
    band = slab[:CY]
    for step in range(1, reach_y):
        band = band + passed_along(slab[step * CY : (step + 1) * CY], "col", step)
    density_yx = band[:, :CX]
    for step in range(1, reach_x):
        density_yx = density_yx + passed_along(band[:, step * CX : (step + 1) * CX], "row", step)
    density = jnp.transpose(density_yx, (1, 0, 2))
    grid_rows = CX * lax.axis_size("row")
    grid_cols = CY * lax.axis_size("col")
    cos_z, sin_z = tables(NZ)
    rho_real = jnp.einsum("yxz,zk->xky", density_yx, cos_z, precision=HIGHEST)
    rho_imag = -jnp.einsum("yxz,zk->xky", density_yx, sin_z, precision=HIGHEST)
    spectrum = lax.all_to_all(
        jnp.stack([rho_real, rho_imag]), "col", split_axis=2, concat_axis=3, tiled=True
    )
    cos_y, sin_y = tables(grid_cols)
    spec_real, spec_imag = along_last(spectrum[0], spectrum[1], cos_y, sin_y, -1.0)
    spectrum = lax.all_to_all(
        jnp.stack([spec_real, spec_imag]), "row", split_axis=2, concat_axis=1, tiled=True
    )
    cos_x, sin_x = tables(grid_rows)
    spec_real, spec_imag = along_first(spectrum[0], spectrum[1], cos_x, sin_x, -1.0)
    depth = NZ // lax.axis_size("col")
    thin_depth = depth // lax.axis_size("row")
    z_index = (
        lax.axis_index("col") * depth
        + lax.axis_index("row") * thin_depth
        + lax.iota(jnp.int32, thin_depth)
    )
    k_square = (
        wave_square(grid_rows, lax.iota(jnp.int32, grid_rows))[:, None, None]
        + wave_square(grid_cols, lax.iota(jnp.int32, grid_cols))[None, None, :]
        + wave_square(NZ, z_index)[None, :, None]
    )
    factor = jnp.where(k_square > 0, SCREEN / (k_square + SCREEN), 0.0)
    spec_real, spec_imag = along_first(spec_real * factor, spec_imag * factor, cos_x, sin_x, 1.0)
    spectrum = lax.all_to_all(
        jnp.stack([spec_real, spec_imag]), "row", split_axis=1, concat_axis=2, tiled=True
    )
    spec_real, spec_imag = along_last(spectrum[0], spectrum[1], cos_y, sin_y, 1.0)
    spectrum = lax.all_to_all(
        jnp.stack([spec_real, spec_imag]), "col", split_axis=3, concat_axis=2, tiled=True
    )
    hartree = jnp.einsum("xky,kz->xyz", spectrum[0], cos_z, precision=HIGHEST) - jnp.einsum(
        "xky,kz->xyz", spectrum[1], sin_z, precision=HIGHEST
    )
    hartree = hartree / float(grid_rows * grid_cols * NZ)
    return (filtered, density, hartree)


def solution(mesh):
    return jax.shard_map(
        shards,
        mesh=mesh,
        in_specs=(
            P(("row", "col"), None, None, None),
            P(("row", "col"), None, None),
            P(("row", "col"), None),
            P(("row", "col")),
            P(("row", "col")),
        ),
        out_specs=(
            P(("row", "col"), None, None, None),
            P("row", "col", None),
            P("row", "col", None),
        ),
        check_vma=False,
    )
```

profile of v0, /device:TPU:0, one launch (start us, length us, event | category | flops | bytes accessed | tf_op | source)
XLA Modules:
  0.0 535.3 jit_solution(7600004614118654446)
XLA Ops:
  3.2 3.5 slice_bitcast_fusion.5
  8.1 22.6 %while.32 = (s32[]{:T(128)}, bf16[8,48,2304]{2,1,0:T(8,128)(2,1)}, f32[48,2304]{1,0:T(8,128)S(1)}, s32[]{:T(128)}, f32[48,2304]{1,0:T(8,128)S(1)}, /*index=5*/bf...) while((s32[]{:T(128)}, bf16[8,48,2304]{2,1,0:T(8,128)(2,1)}, ...), condition=%wide.region_5.6_spmd, body=%wide.region_3.5_spmd.sunk | while | flops 13174278 | bytes 60521680 | solution.py:67
  32.1 17.6 %while.31 = (s32[]{:T(128)}, bf16[8,48,2304]{2,1,0:T(8,128)(2,1)}, f32[48,2304]{1,0:T(8,128)S(1)}, s32[]{:T(128)}, f32[48,2304]{1,0:T(8,128)S(1)}, /*index=5*/bf...) while((s32[]{:T(128)}, bf16[8,48,2304]{2,1,0:T(8,128)(2,1)}, ...), condition=%wide.region_2.3_spmd, body=%wide.region_0.2_spmd.sunk | while | flops 13174278 | bytes 60521680 | solution.py:67
  54.6 4.1 broadcast_in_dim.61
  58.7 28.9 %dynamic_update_slice.18 = f32[56,64,560]{2,0,1:T(8,128)} dynamic-update-slice(f32[56,64,560]{2,0,1:T(8,128)} %broadcast_in_dim.61, f32[48,48,48]{2,0,1:T(8,128)S(1)} %bitcast.206, s32[]{:T(128)S(6)} %select_n.359, s32[]{:T(128)S(6)} %select_n.360, s32[]{:T(128)S(6)} %select_n.361) | dynamic-update-slice | bytes 884740 | tf_op jit(solution)/shard_map/dynamic_update_slice | solution.py:72
  87.6 6.9 %slice.757 = f32[56,64,512]{2,0,1:T(8,128)} slice(f32[56,64,560]{2,0,1:T(8,128)} %dynamic_update_slice.18), slice={[0:56], [0:64], [0:512]} | slice | bytes 14680064 | tf_op jit(solution)/shard_map/slice | solution.py:77
  96.8 10.4 %scatter-add.4 = f32[56,64,512]{2,0,1:T(8,128)} dynamic-update-slice(f32[56,64,512]{2,0,1:T(8,128)} %slice.757, f32[56,64,48]{2,0,1:T(8,128)S(1)} %slice_add_fusion, s32[]{:T(128)} %constant.351.clone.1, s32[]{:T(128)} %constant.351.clone.1, s32[]{:T(128)} %constant.351.clone.1) | dynamic-update-slice | bytes 1376260 | tf_op jit(solution)/shard_map/scatter-add | solution.py:78
  107.1 3.5 fusion.364
  110.7 4.9 collective-permute-start.4
  115.6 114.4 %collective-permute-start.3 = (f32[8,64,512]{2,0,1:T(8,128)S(1)}, f32[8,64,512]{2,0,1:T(8,128)S(1)}, u32[]{:S(2)}, u32[]{:S(2)}) collective-permute-start(f32[8,64,512]{2,0,1:T(8,128)S(1)} %get-tuple-element.358), channel_id=1, source_target_pairs={{0,4},{1,5},{2,6},{3,7},{4,0},{5,1},{6,2},{7,3},{8,12},{9,13},{10,... | collective-permute-start | bytes 3145736 | tf_op jit(solution)/shard_map/ppermute | solution.py:23
  230.1 2.8 collective-permute-start.2
  232.9 2.9 collective-permute-start.1
  235.8 152.1 %collective-permute-done.3 = f32[8,64,512]{2,0,1:T(8,128)S(1)} collective-permute-done((f32[8,64,512]{2,0,1:T(8,128)S(1)}, f32[8,64,512]{2,0,1:T(8,128)S(1)}, u32[]{:S(2)}, u32[]{:S(2)}) %collective-permute-start.3) | collective-permute-done | bytes 1048608 | tf_op jit(solution)/shard_map/ppermute | solution.py:23
  391.2 5.6 %collective-permute-done.8 = f32[8,16,512]{2,0,1:T(8,128)S(1)} collective-permute-done((f32[8,16,512]{2,0,1:T(8,128)S(1)}, f32[8,16,512]{2,0,1:T(8,128)S(1)}, u32[]{:S(2)}, u32[]{:S(2)}) %collective-permute-start.8) | collective-permute-done | bytes 262176 | tf_op jit(solution)/shard_map/ppermute | solution.py:23
  396.9 6.3 %collective-permute-done.7 = f32[8,16,512]{2,0,1:T(8,128)S(1)} collective-permute-done((f32[8,16,512]{2,0,1:T(8,128)S(1)}, f32[8,16,512]{2,0,1:T(8,128)S(1)}, u32[]{:S(2)}, u32[]{:S(2)}) %collective-permute-start.7) | collective-permute-done | bytes 262176 | tf_op jit(solution)/shard_map/ppermute | solution.py:23
  404.0 5.1 fusion.154
  409.1 5.0 convolution_bitcast_fusion
  414.2 3.7 copy.73
  417.8 4.4 reshape.135
  422.2 5.3 all-to-all-start
  427.5 13.1 %all-to-all-done = f32[8,1,16384]{2,1,0:T(1,128)S(1)} async-done(((f32[8,1,16384]{2,1,0:T(1,128)}), f32[8,1,16384]{2,1,0:T(1,128)S(1)}, u32[]{:S(2)}, u32[]{:S(2)}) %all-to-all-start) | async-done | bytes 524320 | tf_op jit(solution)/shard_map/all_to_all | solution.py:154
  443.1 3.4 reshape.136
  446.5 3.2 copy.111
  456.2 3.7 all-to-all-start.1
  460.1 8.7 %all-to-all-done.1 = f32[4,1,32768]{2,1,0:T(1,128)S(1)} async-done(((f32[4,1,32768]{2,1,0:T(1,128)}), f32[4,1,32768]{2,1,0:T(1,128)S(1)}, u32[]{:S(2)}, u32[]{:S(2)}) %all-to-all-start.1) | async-done | bytes 524320 | tf_op jit(solution)/shard_map/all_to_all | solution.py:159
  479.4 11.7 %all_to_all.60 = f32[4,1,32768]{2,1,0:T(1,128)S(1)} all-to-all(f32[4,1,32768]{2,1,0:T(1,128)S(1)} %reshape.139), channel_id=1, replica_groups=mesh['row'=4,'col'=8] {'row'}, dimensions={0} | all-to-all | bytes 1048576 | tf_op jit(solution)/shard_map/all_to_all | solution.py:178
  498.8 2.8 reshape.141
  501.6 4.3 all-to-all-start.3
  508.0 12.3 %all-to-all-done.3 = f32[8,1,16384]{2,1,0:T(1,128)} async-done(((f32[8,1,16384]{2,1,0:T(1,128)}), f32[8,1,16384]{2,1,0:T(1,128)}, u32[]{:S(2)}, u32[]{:S(2)}) %all-to-all-start.3) | async-done | bytes 524320 | tf_op jit(solution)/shard_map/all_to_all | solution.py:182
  520.3 2.9 reduce.5
  524.6 4.9 fusion.166
  529.7 5.4 %fusion.155 = f32[16,8,512]{2,1,0:T(8,128)} fusion(f32[16,8,512]{2,1,0:T(8,128)S(1)} %fusion.166, f32[16,512,8]{1,2,0:T(8,128)S(1)} %squeeze.74), kind=kOutput, calls=%fused_computation.193 | convolution fusion | flops 406454272 | bytes 786432 | tf_op jit(solution)/shard_map/xky,kz->xyz/dot_general | solution.py:185
  (199 shorter events, 76.7 us)
Async XLA Ops:
  32.1 17.6 %copy-start.4 = (s32[2]{0:T(128)S(1)}, s32[2]{0:T(128)}, u32[]{:S(2)}) copy-start(s32[2]{0:T(128)} %param.14) | copy-start | bytes 28
  49.9 0.8 copy-start.3
  110.7 125.1 %collective-permute-start.5 = (f32[8,64,512]{2,0,1:T(8,128)S(1)}, f32[8,64,512]{2,0,1:T(8,128)S(1)}, u32[]{:S(2)}, u32[]{:S(2)}) collective-permute-start(f32[8,64,512]{2,0,1:T(8,128)S(1)} %get-tuple-element.356), channel_id=1, source_target_pairs={{0,6},{1,7},{2,0},{3,1},{4,2},{5,3},{6,4},{7,5},{8,14},{9,15},{10,... | collective-permute-start | bytes 3145736 | tf_op jit(solution)/shard_map/ppermute | solution.py:23
  110.7 125.1 %collective-permute-start.4 = (f32[8,64,512]{2,0,1:T(8,128)S(1)}, f32[8,64,512]{2,0,1:T(8,128)S(1)}, u32[]{:S(2)}, u32[]{:S(2)}) collective-permute-start(f32[8,64,512]{2,0,1:T(8,128)S(1)} %get-tuple-element.357), channel_id=1, source_target_pairs={{0,5},{1,6},{2,7},{3,0},{4,1},{5,2},{6,3},{7,4},{8,13},{9,14},{10,... | collective-permute-start | bytes 3145736 | tf_op jit(solution)/shard_map/ppermute | solution.py:23
  115.6 272.3 %collective-permute-start.3 = (f32[8,64,512]{2,0,1:T(8,128)S(1)}, f32[8,64,512]{2,0,1:T(8,128)S(1)}, u32[]{:S(2)}, u32[]{:S(2)}) collective-permute-start(f32[8,64,512]{2,0,1:T(8,128)S(1)} %get-tuple-element.358), channel_id=1, source_target_pairs={{0,4},{1,5},{2,6},{3,7},{4,0},{5,1},{6,2},{7,3},{8,12},{9,13},{10,... | collective-permute-start | bytes 3145736 | tf_op jit(solution)/shard_map/ppermute | solution.py:23
  230.1 157.8 %collective-permute-start.2 = (f32[8,64,512]{2,0,1:T(8,128)S(1)}, f32[8,64,512]{2,0,1:T(8,128)S(1)}, u32[]{:S(2)}, u32[]{:S(2)}) collective-permute-start(f32[8,64,512]{2,0,1:T(8,128)S(1)} %get-tuple-element.359), channel_id=1, source_target_pairs={{0,3},{1,4},{2,5},{3,6},{4,7},{5,0},{6,1},{7,2},{8,11},{9,12},{10,... | collective-permute-start | bytes 3145736 | tf_op jit(solution)/shard_map/ppermute | solution.py:23
  232.9 155.0 %collective-permute-start.1 = (f32[8,64,512]{2,0,1:T(8,128)S(1)}, f32[8,64,512]{2,0,1:T(8,128)S(1)}, u32[]{:S(2)}, u32[]{:S(2)}) collective-permute-start(f32[8,64,512]{2,0,1:T(8,128)S(1)} %get-tuple-element.360), channel_id=1, source_target_pairs={{0,2},{1,3},{2,4},{3,5},{4,6},{5,7},{6,0},{7,1},{8,10},{9,11},{10,... | collective-permute-start | bytes 3145736 | tf_op jit(solution)/shard_map/ppermute | solution.py:23
  235.8 152.1 %collective-permute-start = (f32[8,64,512]{2,0,1:T(8,128)S(1)}, f32[8,64,512]{2,0,1:T(8,128)S(1)}, u32[]{:S(2)}, u32[]{:S(2)}) collective-permute-start(f32[8,64,512]{2,0,1:T(8,128)S(1)} %get-tuple-element.355), channel_id=1, source_target_pairs={{0,1},{1,2},{2,3},{3,4},{4,5},{5,6},{6,7},{7,0},{8,9},{9,10},{10,1... | collective-permute-start | bytes 3145736 | tf_op jit(solution)/shard_map/ppermute | solution.py:23
  390.1 6.8 %collective-permute-start.8 = (f32[8,16,512]{2,0,1:T(8,128)S(1)}, f32[8,16,512]{2,0,1:T(8,128)S(1)}, u32[]{:S(2)}, u32[]{:S(2)}) collective-permute-start(f32[8,16,512]{2,0,1:T(8,128)S(1)} %get-tuple-element.372), channel_id=1, source_target_pairs={{0,24},{8,0},{16,8},{24,16},{1,25},{9,1},{17,9},{25,17},{2,26},{10... | collective-permute-start | bytes 786440 | tf_op jit(solution)/shard_map/ppermute | solution.py:23
  390.2 13.0 %collective-permute-start.7 = (f32[8,16,512]{2,0,1:T(8,128)S(1)}, f32[8,16,512]{2,0,1:T(8,128)S(1)}, u32[]{:S(2)}, u32[]{:S(2)}) collective-permute-start(f32[8,16,512]{2,0,1:T(8,128)S(1)} %get-tuple-element.373), channel_id=1, source_target_pairs={{0,16},{8,24},{16,0},{24,8},{1,17},{9,25},{17,1},{25,9},{2,18},{10... | collective-permute-start | bytes 786440 | tf_op jit(solution)/shard_map/ppermute | solution.py:23
  391.1 12.8 %collective-permute-start.6 = (f32[8,16,512]{2,0,1:T(8,128)S(1)}, f32[8,16,512]{2,0,1:T(8,128)S(1)}, u32[]{:S(2)}, u32[]{:S(2)}) collective-permute-start(f32[8,16,512]{2,0,1:T(8,128)S(1)} %get-tuple-element.371), channel_id=1, source_target_pairs={{0,8},{8,16},{16,24},{24,0},{1,9},{9,17},{17,25},{25,1},{2,10},{10... | collective-permute-start | bytes 786440 | tf_op jit(solution)/shard_map/ppermute | solution.py:23
  403.9 5.1 copy-start.2
  422.2 18.4 %all-to-all-start = ((f32[8,1,16384]{2,1,0:T(1,128)}), f32[8,1,16384]{2,1,0:T(1,128)S(1)}, u32[]{:S(2)}, u32[]{:S(2)}) async-start(f32[8,1,16384]{2,1,0:T(1,128)} %reshape.135), calls=%async_computation | async-start | bytes 1048576 | tf_op jit(solution)/shard_map/all_to_all | solution.py:154
  456.2 12.5 %all-to-all-start.1 = ((f32[4,1,32768]{2,1,0:T(1,128)}), f32[4,1,32768]{2,1,0:T(1,128)S(1)}, u32[]{:S(2)}, u32[]{:S(2)}) async-start(f32[4,1,32768]{2,1,0:T(1,128)} %reshape.137), calls=%async_computation.1 | async-start | bytes 1048576 | tf_op jit(solution)/shard_map/all_to_all | solution.py:159
  497.0 9.0 %copy-start.1 = (bf16[8,48,2304]{2,1,0:T(8,128)(2,1)S(1)}, bf16[8,48,2304]{2,1,0:T(8,128)(2,1)}, u32[]{:S(2)}) copy-start(bf16[8,48,2304]{2,1,0:T(8,128)(2,1)} %get-tuple-element.240) | copy-start | bytes 5308420
  498.8 7.2 %copy-start = (bf16[8,48,2304]{2,1,0:T(8,128)(2,1)S(1)}, bf16[8,48,2304]{2,1,0:T(8,128)(2,1)}, u32[]{:S(2)}) copy-start(bf16[8,48,2304]{2,1,0:T(8,128)(2,1)} %get-tuple-element.239) | copy-start | bytes 5308420
  501.6 18.7 %all-to-all-start.3 = ((f32[8,1,16384]{2,1,0:T(1,128)}), f32[8,1,16384]{2,1,0:T(1,128)}, u32[]{:S(2)}, u32[]{:S(2)}) async-start(f32[8,1,16384]{2,1,0:T(1,128)} %reshape.141), calls=%async_computation.3 | async-start | bytes 1048576 | tf_op jit(solution)/shard_map/all_to_all | solution.py:182
where the time goes:
time: 527 us; the launch traced here: 535 us
  waiting for transfers between devices  199 us (38%)
  starting transfers between devices  140 us (27%)
  local copies, waits for them, and re-layouts  101 us (19%)
  other arithmetic  38.5 us (7%)
  matrix products  33.7 us (6%)
  blocking collectives  11.7 us (2%)
  loops' own time  7.55 us (1%)
    ppermute x9, waiting for transfers between devices, passed_along(): lax.ppermute(value, axis, [(i, (i + by) % peers) for i in range(peers)])  165 us
    ppermute x9, starting transfers between devices, passed_along(): lax.ppermute(value, axis, [(i, (i + by) % peers) for i in range(peers)])  126 us
    dynamic_update_slice x1, local copies, waits for them, and re-layouts, place_all(): lax.dynamic_update_slice(slab, jnp.transpose(cubes[0], (1, 0, 2)), start)  28.9 us
    unnamed x18, local copies, waits for them, and re-layouts  14.2 us
    all_to_all x1, waiting for transfers between devices, shards(): lax.all_to_all(jnp.stack([rho_real, rho_imag]), 'col', split_axis=2, conc...  13.1 us
    all_to_all x1, waiting for transfers between devices, shards(): lax.all_to_all(jnp.stack([spec_real, spec_imag]), 'col', split_axis=3, co...  12.3 us
    all_to_all x1, blocking collectives, shards(): lax.all_to_all(jnp.stack([spec_real, spec_imag]), 'row', split_axis=1, co...  11.7 us
  transfers between devices with their start and end apart: 12, of which 7 were waited for; matrix products, arithmetic and copies ran while one was open for 0% of the time, Pallas kernels for 0%

commit v1 on v0

v1 whole, which is shorter than its diff:
```python
import functools
import math

import jax
import jax.numpy as jnp
import ml_dtypes
import numpy as np
from jax import lax
from jax.experimental import pallas as pl
from jax.experimental.pallas import tpu as pltpu
from jax.sharding import PartitionSpec as P

CENTER = 5.25
HALF_WIDTH = 3.75
SCREEN = 0.0025
LANES = 128
HALF = 64
GROUP = 8
HIGHEST = lax.Precision.HIGHEST
BF16 = jnp.bfloat16
F32 = jnp.float32
TILES = ((0, 0), (1, 0), (1, 1), (2, 1), (2, 2), (3, 2))


def real_basis(length):
    m = np.arange(length)[:, None]
    n = np.arange(length)[None, :]
    angle = 2 * np.pi * ((m * n) % length) / length
    rows = np.where(m <= length // 2, np.cos(angle), np.sin(angle))
    weight = np.where((m == 0) | (2 * m == length), 1.0, 2.0) / length
    return rows * np.sqrt(weight)


def split_table(table):
    high = table.astype(np.float32).astype(ml_dtypes.bfloat16)
    low = (table - high.astype(np.float64)).astype(np.float32).astype(ml_dtypes.bfloat16)
    return high, low


def split2(value):
    high = value.astype(BF16)
    return high, (value - high.astype(F32)).astype(BF16)


def dot(a, b, dims=((1,), (0,))):
    return lax.dot_general(a, b, (dims, ((), ())), preferred_element_type=F32)


def dot3(a, b, dims=((1,), (0,))):
    return dot(a[0], b[0], dims) + (dot(a[0], b[1], dims) + dot(a[1], b[0], dims))


def move_matrix(pair, tile, side, inward):
    shape = (2 * LANES, 2 * LANES)
    boxed = lax.broadcasted_iota(jnp.int32, shape, 1 if inward else 0)
    flat = lax.broadcasted_iota(jnp.int32, shape, 0 if inward else 1)
    y = 2 * pair + boxed // LANES
    fragment = boxed % LANES // HALF
    z = boxed % HALF
    hit = (fragment == flat // LANES) & (z < side)
    hit = hit & (y * side + z == tile * LANES + flat % LANES)
    return jnp.where(hit, 1.0, 0.0).astype(BF16)


def filter_kernel(
    reach,
    mesh_sizes,
    own,
    corners_ref,
    signs_ref,
    counts_ref,
    orb_ref,
    pot_ref,
    out_ref,
    send_ref,
    even,
    odd,
    coef,
    moves,
    packed,
    slab,
    scales,
):
    _, orbs, side, _ = orb_ref.shape
    rows = orbs * side
    groups = side // GROUP
    lane = lax.broadcasted_iota(jnp.int32, (orbs, LANES), 1)
    for index, (pair, tile) in enumerate(TILES):
        moves[index] = move_matrix(pair, tile, side, True)
    for field in (even, odd):
        zeros = jnp.zeros((field.shape[1], LANES), F32)
        field[0] = zeros
        field[side + 1] = zeros
        edge = jnp.zeros((orbs, LANES), F32)

        def clear(y, carry):
            field[y, pl.ds(0, orbs), :] = edge
            field[y, pl.ds(orbs * (side + 1), orbs), :] = edge
            return carry

        lax.fori_loop(1, side + 1, clear, 0)

    def spread(parts):
        results = []
        for pair in range(GROUP // 2):
            total = None
            for index, (p, tile) in enumerate(TILES):
                if p == pair:
                    term = dot(parts[tile], moves[index])
                    total = term if total is None else total + term
            results.append(total)
        return results

    def load_group(g, carry):
        base = g * (GROUP * side)
        parts = []
        pot_parts = []
        for tile in range(3):
            cols = pl.ds(pl.multiple_of(base + tile * LANES, LANES), LANES)
            parts.append(
                jnp.concatenate([orb_ref[f, :, :, cols].reshape(rows, LANES) for f in range(2)], 1)
            )
            pot = jnp.concatenate([pot_ref[f, :, cols] for f in range(2)], 1)
            first = pot.astype(BF16)
            rest = pot - first.astype(F32)
            second = rest.astype(BF16)
            third = (rest - second.astype(F32)).astype(BF16)
            pot_parts.append(jnp.concatenate([first, second, third], 0))
        fields = spread(parts)
        pots = spread(pot_parts)
        for pair in range(GROUP // 2):
            for k in range(2):
                y = g * GROUP + 2 * pair + k
                cols = slice(k * LANES, (k + 1) * LANES)
                for orb in range(orbs):
                    even[y + 1, pl.ds(orbs + orb, side, stride=orbs), :] = fields[pair][
                        orb * side : (orb + 1) * side, cols
                    ]
                stack = pots[pair][:, cols]
                pot = (stack[:side] + stack[side : 2 * side]) + stack[2 * side :]
                coef[y] = (pot + (3.0 - CENTER)) * (2.0 / HALF_WIDTH)
        return carry

    lax.fori_loop(0, groups, load_group, 0)

    coupling = jnp.where(lane % HALF < side, 1.0 / HALF_WIDTH, 0.0).astype(F32)

    def step(now, other, first, last):
        def plane(y, total):
            squares = None
            before = now[y, pl.ds(0, orbs), :]
            here = now[y, pl.ds(orbs, orbs), :]
            for x in range(side):
                row = pl.ds(orbs * (x + 1), orbs)
                after = now[y, pl.ds(orbs * (x + 2), orbs), :]
                beside = (before + after) + (now[y - 1, row, :] + now[y + 1, row, :])
                beside = beside + (
                    pltpu.roll(here, 1, axis=1) + pltpu.roll(here, LANES - 1, axis=1)
                )
                result = coef[y - 1, pl.ds(x, 1), :] * here - coupling * beside
                result = 0.5 * result if first else result - other[y, row, :]
                other[y, row, :] = result
                if last:
                    square = result * result
                    squares = square if squares is None else squares + square
                before, here = here, after
            return total + squares if last else total

        return lax.fori_loop(1, side + 1, plane, jnp.zeros((orbs, LANES), F32))

    step(even, odd, True, False)
    step(odd, even, False, False)
    step(even, odd, False, False)
    step(odd, even, False, False)
    step(even, odd, False, False)
    total = step(odd, even, False, True)

    left = lane < HALF
    sums = jnp.where(
        left,
        jnp.sum(jnp.where(left, total, 0.0), axis=1, keepdims=True),
        jnp.sum(jnp.where(left, 0.0, total), axis=1, keepdims=True),
    )
    shifted = sums * (1.0 / side**3) + 1e-6
    scale = lax.rsqrt(shifted)
    scale = scale * (1.5 - 0.5 * shifted * scale * scale)
    live = lax.broadcasted_iota(jnp.int32, (orbs, LANES), 0) < jnp.where(
        left, counts_ref[0], counts_ref[1]
    )
    scales[...] = jnp.where(live, scale, 0.0)
    sign = jnp.where(left, signs_ref[0], signs_ref[1]).astype(F32)[:1]

    for index, (pair, tile) in enumerate(TILES):
        moves[index] = move_matrix(pair, tile, side, False)
    row_index, col_index = own()
    own_x = corners_ref[0, 0] - row_index * reach[2]
    own_y = corners_ref[0, 1] - col_index * reach[3]
    slab[...] = jnp.zeros_like(slab)
    pad = jnp.zeros((slab.shape[1] - side, LANES), F32)

    def store_group(g, carry):
        for k in range(GROUP):
            y = g * GROUP + k
            box = jnp.zeros((side, LANES), F32)
            for orb in range(orbs):
                q = even[y + 1, pl.ds(orbs + orb, side, stride=orbs), :] * scales[pl.ds(orb, 1), :]
                packed[pl.ds(orb * side, side), pl.ds(k * LANES, LANES)] = q.astype(BF16)
                box = box + q * q
            box = box * sign
            box = box + pltpu.roll(box, HALF, axis=1)
            slab[y + own_y] = pltpu.roll(jnp.concatenate([box, pad], 0), own_x, axis=0)
        base = g * (GROUP * side)
        for tile in range(3):
            flat = None
            for index, (pair, t) in enumerate(TILES):
                if t == tile:
                    term = dot(packed[:, pl.ds(2 * pair * LANES, 2 * LANES)], moves[index])
                    flat = term if flat is None else flat + term
            cols = pl.ds(pl.multiple_of(base + tile * LANES, LANES), LANES)
            for f in range(2):
                out_ref[f, :, :, cols] = (
                    flat[:, f * LANES : (f + 1) * LANES].astype(BF16).reshape(orbs, side, LANES)
                )
        return carry

    lax.fori_loop(0, groups, store_group, 0)

    cut = lane[:8]

    def pack(i, carry):
        for j in range(reach[1]):
            target = (row_index + i) % mesh_sizes[0] * mesh_sizes[1]
            target = target + (col_index + j) % mesh_sizes[1]
            for part in range(reach[2] // 8):
                xs = pl.ds(pl.multiple_of(i * reach[2] + part * 8, 8), 8)
                v = []
                for k in range(GROUP):
                    line = slab[j * GROUP + k, xs, :]
                    shift = k * side % LANES
                    v.append(line if shift == 0 else pltpu.roll(line, shift, axis=1))
                tiles = (
                    jnp.where(cut < 48, v[0], jnp.where(cut < 96, v[1], v[2])),
                    jnp.where(
                        cut < 16, v[2], jnp.where(cut < 64, v[3], jnp.where(cut < 112, v[4], v[5]))
                    ),
                    jnp.where(cut < 32, v[5], jnp.where(cut < 80, v[6], v[7])),
                )
                for t in range(3):
                    send_ref[target, pl.ds((part * 3 + t) * 8, 8), :] = tiles[t]
        return carry

    lax.fori_loop(0, reach[0], pack, 0)


def gather_kernel(reach, mesh_sizes, own, side, starts_ref, got_ref, high_ref, low_ref, dens_ref, spec_ref, acc):
    row_index, col_index = own()
    acc[...] = jnp.zeros_like(acc)
    depth = acc.shape[0]
    lane = lax.broadcasted_iota(jnp.int32, (8, LANES), 1)

    def add(step, carry):
        i = step // reach[1]
        j = step % reach[1]
        source = (row_index + mesh_sizes[0] - i) % mesh_sizes[0] * mesh_sizes[1]
        source = source + (col_index + mesh_sizes[1] - j) % mesh_sizes[1]
        start = starts_ref[source]
        tile = start // LANES
        inner = start % LANES
        following = (tile + 1) % depth
        here = (lane >= inner) & (lane < inner + side)
        wrapped = lane < inner + side - LANES
        for part in range(reach[2] // 8):
            t0, t1, t2 = (got_ref[source, pl.ds((part * 3 + t) * 8, 8), :] for t in range(3))
            joined = (
                t0, t0, jnp.where(lane >= 96, t0, t1), t1, t1, jnp.where(lane >= 112, t1, t2), t2, t2
            )
            for k in range(GROUP):
                moved = pltpu.roll(joined[k], (inner + (LANES - k * side % LANES)) % LANES, axis=1)
                rows = pl.ds(part * 64 + k, 8, stride=GROUP)
                acc[tile, rows, :] += jnp.where(here, moved, 0.0)
                acc[following, rows, :] += jnp.where(wrapped, moved, 0.0)
        return carry

    lax.fori_loop(0, reach[0] * reach[1], add, 0)
    whole = jnp.concatenate([acc[t] for t in range(depth)], 1)
    dens_ref[...] = whole.reshape(dens_ref.shape)
    spec_ref[...] = dot3((high_ref[...], low_ref[...]), split2(whole), ((1,), (1,)))


def screen_kernel(rows, cols, own, sizes, got_ref, vh, vl, wh, wl, out_ref):
    row_index, col_index = own()
    thin = got_ref.shape[1]
    nx, ny, nz = sizes
    cx, cy = nx // rows, ny // cols
    v = (vh[...], vl[...])
    w = (wh[...], wl[...])
    by_x = jnp.concatenate(
        [jnp.concatenate([got_ref[r * cols + c] for r in range(rows)], 1) for c in range(cols)], 0
    )
    by_x = dot3(split2(by_x), v)
    by_y = jnp.concatenate(
        [
            jnp.concatenate(
                [
                    by_x[c * thin : (c + 1) * thin, r * LANES : (r + 1) * LANES]
                    for c in range(cols)
                ],
                1,
            )
            for r in range(rows)
        ],
        0,
    )
    by_y = dot3(split2(by_y), w)

    def square(index, length):
        signed = jnp.where(index <= length // 2, index, index - length).astype(F32)
        wave = signed * (2 * math.pi / length)
        return wave * wave

    row = lax.broadcasted_iota(jnp.int32, by_y.shape, 0)
    lane = lax.broadcasted_iota(jnp.int32, by_y.shape, 1)
    kz = (row_index * cols + col_index) * thin + row % thin
    kx = row // thin * cx + lane % LANES // cy
    ky = lane // LANES * cy + lane % cy
    k_square = (square(kx, nx) + square(ky, ny)) + square(kz, nz)
    factor = jnp.where(k_square > 0, SCREEN / (k_square + SCREEN), 0.0)
    by_y = dot3(split2(by_y * factor), w, ((1,), (1,)))
    by_x = jnp.concatenate(
        [
            jnp.concatenate(
                [
                    by_y[r * thin : (r + 1) * thin, c * LANES : (c + 1) * LANES]
                    for r in range(rows)
                ],
                1,
            )
            for c in range(cols)
        ],
        0,
    )
    by_x = dot3(split2(by_x), v, ((1,), (1,)))
    for r in range(rows):
        for c in range(cols):
            out_ref[r * cols + c] = by_x[c * thin : (c + 1) * thin, r * LANES : (r + 1) * LANES]


def back_kernel(got_ref, high_ref, low_ref, out_ref):
    spec = jnp.transpose(got_ref[...], (1, 0))
    out_ref[...] = dot3(split2(spec), (high_ref[...], low_ref[...])).reshape(out_ref.shape)


def shards(orbitals, potential_boxes, corners, signs, counts, *, rows, cols, out_block):
    cx, cy, nz = out_block
    frags, orbs, side, _ = orbitals.shape
    peers = rows * cols
    nx, ny = cx * rows, cy * cols
    thin = nz // peers
    reach = ((cx + side - 2) // cx + 1, (cy + side - 2) // cy + 1, cx, cy)
    mesh_sizes = (rows, cols)

    def own():
        return lax.axis_index("row"), lax.axis_index("col")

    vmem = pl.BlockSpec(memory_space=pltpu.VMEM)
    smem = pl.BlockSpec(memory_space=pltpu.SMEM)
    params = pltpu.CompilerParams(vmem_limit_bytes=52 * 2**20)
    starts = lax.all_gather(corners[0, 2], ("row", "col"))
    block_rows = cx // 8 * 3 * 8
    filtered, send = pl.pallas_call(
        functools.partial(filter_kernel, reach, mesh_sizes, own),
        out_shape=(
            jax.ShapeDtypeStruct(orbitals.shape, BF16),
            jax.ShapeDtypeStruct((peers, block_rows, LANES), F32),
        ),
        in_specs=[smem] * 3 + [vmem] * 2,
        out_specs=(vmem, vmem),
        scratch_shapes=[
            pltpu.VMEM((side + 2, (side + 2) * orbs, LANES), F32),
            pltpu.VMEM((side + 2, (side + 2) * orbs, LANES), F32),
            pltpu.VMEM((side, side, LANES), F32),
            pltpu.VMEM((len(TILES), 2 * LANES, 2 * LANES), BF16),
            pltpu.VMEM((orbs * side, GROUP * LANES), BF16),
            pltpu.VMEM((reach[1] * cy, reach[0] * cx, LANES), F32),
            pltpu.VMEM((orbs, LANES), F32),
        ],
        compiler_params=params,
    )(corners, signs, counts, orbitals, potential_boxes)
    got = lax.all_to_all(send, ("row", "col"), 0, 0, tiled=True)
    z_high, z_low = split_table(real_basis(nz))
    density, spec = pl.pallas_call(
        functools.partial(gather_kernel, reach, mesh_sizes, own, side),
        out_shape=(
            jax.ShapeDtypeStruct(out_block, F32),
            jax.ShapeDtypeStruct((nz, cx * cy), F32),
        ),
        in_specs=[smem] + [vmem] * 3,
        out_specs=(vmem, vmem),
        scratch_shapes=[pltpu.VMEM((nz // LANES, cx * cy, LANES), F32)],
        compiler_params=params,
    )(starts, got, z_high, z_low)
    spec = spec.reshape(peers, thin, cx * cy)
    spec = lax.all_to_all(spec, ("row", "col"), 0, 0, tiled=True)
    x_basis, y_basis = real_basis(nx), real_basis(ny)
    if thin % 8 == 0 and ny * cx <= 1024:
        x_table = np.kron(x_basis.T, np.eye(cy))
        y_table = np.einsum("mcy,xw->cxymw", y_basis.reshape(ny, cols, cy), np.eye(cx))
        y_table = y_table.reshape(cols * cx * cy, cols, cy, cx).transpose(0, 1, 3, 2)
        y_table = y_table.reshape(cols * cx * cy, cols * cx * cy)
        spec = pl.pallas_call(
            functools.partial(screen_kernel, rows, cols, own, (nx, ny, nz)),
            out_shape=jax.ShapeDtypeStruct(spec.shape, F32),
            in_specs=[vmem] * 5,
            out_specs=vmem,
            compiler_params=params,
        )(spec, *split_table(x_table), *split_table(y_table))
    else:
        x_basis, y_basis = x_basis.astype(np.float32), y_basis.astype(np.float32)

        def square(index, length):
            wave = jnp.where(index <= length // 2, index, index - length).astype(F32) * (
                2 * math.pi / length
            )
            return wave * wave

        r, c = own()
        grid = spec.reshape(rows, cols, thin, cx, cy).transpose(2, 0, 3, 1, 4)
        grid = grid.reshape(thin, nx, ny)
        grid = jnp.einsum("kxy,ax,by->kab", grid, x_basis, y_basis, precision=HIGHEST)
        k_square = (
            square(jnp.arange(nx), nx)[None, :, None] + square(jnp.arange(ny), ny)[None, None, :]
        ) + square((r * cols + c) * thin + jnp.arange(thin), nz)[:, None, None]
        grid = grid * jnp.where(k_square > 0, SCREEN / (k_square + SCREEN), 0.0)
        grid = jnp.einsum("kab,ax,by->kxy", grid, x_basis, y_basis, precision=HIGHEST)
        grid = grid.reshape(thin, rows, cx, cols, cy).transpose(1, 3, 0, 2, 4)
        spec = grid.reshape(spec.shape)
    spec = lax.all_to_all(spec, ("row", "col"), 0, 0, tiled=True).reshape(nz, cx * cy)
    hartree = pl.pallas_call(
        back_kernel,
        out_shape=jax.ShapeDtypeStruct(out_block, F32),
        in_specs=[vmem] * 3,
        out_specs=vmem,
        compiler_params=params,
    )(spec, z_high, z_low)
    return (filtered, density, hartree)


def solution(mesh):
    rows, cols = mesh.shape["row"], mesh.shape["col"]
    return jax.shard_map(
        functools.partial(shards, rows=rows, cols=cols, out_block=(16, 8, 512)),
        mesh=mesh,
        in_specs=(
            P(("row", "col"), None, None, None),
            P(("row", "col"), None, None),
            P(("row", "col"), None),
            P(("row", "col")),
            P(("row", "col")),
        ),
        out_specs=(
            P(("row", "col"), None, None, None),
            P("row", "col", None),
            P("row", "col", None),
        ),
        check_vma=False,
    )
```

time: 527 us -> 168 us (0.32); the launches traced: 535 us -> 167 us
  waiting for transfers between devices: 199 us -> 0.01 us
  starting transfers between devices: 140 us -> 7.3 us
  local copies, waits for them, and re-layouts: 101 us -> 5.4 us
  Pallas kernels: 0 us -> 84.5 us
  blocking collectives: 11.7 us -> 69.6 us
  other arithmetic: 38.5 us -> 0 us
  matrix products: 33.7 us -> 0 us
  loops' own time: 7.55 us -> 0 us
    ppermute x9 -> x0, waiting for transfers between devices: 165 us -> none  [passed_along(): lax.ppermute(value, axis, [(i, (i + by) % peers) for i in range(peers)])]
    ppermute x9 -> x0, starting transfers between devices: 126 us -> none  [passed_along(): lax.ppermute(value, axis, [(i, (i + by) % peers) for i in range(peers)])]
    pallas_call x0 -> x4, Pallas kernels: none -> 84.5 us  [the longest x1 69.3 us: shards(): pl.pallas_call(functools.partial(filter_kernel, reach, mesh_sizes, own),...]
    all_gather x0 -> x1, blocking collectives: none -> 41.8 us  [shards(): starts = lax.all_gather(corners[0, 2], ('row', 'col'))]
    all_to_all x3 -> x1, waiting for transfers between devices: 34.1 us -> 0.01 us  [shards(): got = lax.all_to_all(send, ('row', 'col'), 0, 0, tiled=True)]
    dot_general x20 -> x0, matrix products: 33.7 us -> none  [the longest x1 5.39 us: shards(): jnp.einsum('xky,kz->xyz', spectrum[1], sin_z, precision=HIGHEST)]
    dynamic_update_slice x1 -> x0, local copies, waits for them, and re-layouts: 28.9 us -> none  [place_all(): lax.dynamic_update_slice(slab, jnp.transpose(cubes[0], (1, 0, 2)), start)]
    slice x83 -> x1, local copies, waits for them, and re-layouts: 23.5 us -> 0.58 us  [shards(): starts = lax.all_gather(corners[0, 2], ('row', 'col'))]
  transfers between devices with their start and end apart: 12 -> 1, of which waited for: 7 -> 0; matrix products, arithmetic and copies ran while one was open for 0% -> 1% of each run, Pallas kernels for 0% -> 0%
where the time goes in v1:
time: 168 us; the launch traced here: 167 us
  Pallas kernels  84.5 us (50%)
  blocking collectives  69.6 us (41%)
  starting transfers between devices  7.3 us (4%)
  local copies, waits for them, and re-layouts  5.4 us (3%)
    pallas_call x1, Pallas kernels, shards(): pl.pallas_call(functools.partial(filter_kernel, reach, mesh_sizes, own),...  69.3 us
    all_gather x1, blocking collectives, shards(): starts = lax.all_gather(corners[0, 2], ('row', 'col'))  41.8 us
    all_to_all x1, blocking collectives, shards(): spec = lax.all_to_all(spec, ('row', 'col'), 0, 0, tiled=True)  15 us
    all_to_all x1, blocking collectives, shards(): lax.all_to_all(spec, ('row', 'col'), 0, 0, tiled=True).reshape(nz, cx * cy)  12.8 us
    pallas_call x1, Pallas kernels, shards(): pl.pallas_call(functools.partial(gather_kernel, reach, mesh_sizes, own, s...  7.89 us
    all_to_all x1, starting transfers between devices, shards(): got = lax.all_to_all(send, ('row', 'col'), 0, 0, tiled=True)  7.3 us
    pallas_call x1, Pallas kernels, shards(): pl.pallas_call(functools.partial(screen_kernel, rows, cols, own, (nx, ny,...  6.17 us
    unnamed x22, local copies, waits for them, and re-layouts  4.82 us
  transfers between devices with their start and end apart: 1, of which 0 were waited for; matrix products, arithmetic and copies ran while one was open for 1% of the time, Pallas kernels for 0%

profile of v1, /device:TPU:0, one launch (start us, length us, event | category | flops | bytes accessed | tf_op | source)
XLA Modules:
  0.0 167.5 jit_solution(11940212155187823616)
XLA Ops:
  0.6 0.0 copy-start
  0.6 0.0 copy-start.1
  0.7 0.0 copy-start.2
  0.7 1.2 copy-done.2
  1.9 0.0 copy-start.5
  1.9 0.7 copy-done.5
  2.6 0.0 copy-start.7
  2.6 0.7 copy-done.7
  3.2 0.0 copy-start.8
  3.2 0.7 copy-done.8
  3.9 0.0 copy-start.6
  3.9 0.0 copy-start.3
  3.9 0.0 copy-start.4
  3.9 69.3 %shard_map.130 = (bf16[2,8,48,2304]{3,2,1,0:T(8,128)(2,1)}, f32[32,48,128]{2,1,0:T(8,128)}) custom-call(s32[2,3]{1,0:T(2,128)S(1)} %copy-done.5, s32[2]{0:T(128)S(1)} %copy-done.7, s32[2]{0:T(128)S(1)} %copy-done.8, bf16[2,8,48,2304]{3,2,1,0:T(8,128)(2,1)} %orb_ref.1, f32[2,48,2304]{2,1,0:T(8,128)S(1)} %copy-done.2), custom_call_target="tpu_custom_call" | custom-call | tf_op jit(solution)/shard_map/pallas_call | solution.py:370
  73.2 7.3 %all-to-all-start = ((f32[32,48,128]{2,1,0:T(8,128)}), f32[32,48,128]{2,1,0:T(8,128)S(1)}, u32[]{:S(2)}, u32[]{:S(2)}) async-start(f32[32,48,128]{2,1,0:T(8,128)} %get-tuple-element.8), calls=%async_computation | async-start | bytes 1572864 | tf_op jit(solution)/shard_map/all_to_all | solution.py:389
  80.5 0.0 copy-done.6
  80.5 0.6 slice.3
  81.1 0.7 bitcast_dynamic-update-slice_fusion
  81.8 41.8 %all-reduce.starts_ref = s32[32]{0:T(128)S(1)} all-reduce(s32[32]{0:T(128)S(1)} %bitcast_dynamic-update-slice_fusion), channel_id=2, replica_groups=mesh['row'=4,'col'=8] {'row','col'}, use_global_device_ids=true, to_apply=%add | all-reduce | flops 32 | bytes 256 | tf_op jit(solution)/shard_map/all_gather | solution.py:368
  123.6 0.0 all-to-all-done.got_ref
  123.6 0.0 copy-start.9
  123.6 0.9 copy-done.9
  124.5 0.0 copy-done
  124.5 0.0 copy-done.1
  124.5 7.9 %shard_map.131 = (f32[16,8,512]{2,1,0:T(8,128)}, f32[512,128]{1,0:T(8,128)S(1)}) custom-call(s32[32]{0:T(128)S(1)} %all-reduce.starts_ref, f32[32,48,128]{2,1,0:T(8,128)} %copy-done.9, bf16[512,512]{1,0:T(8,128)(2,1)S(1)} %copy-done, bf16[512,512]{1,0:T(8,128)(2,1)S(1)} %copy-done.1), custom_call_target="tpu_custom_call" | custom-call | tf_op jit(solution)/shard_map/pallas_call | solution.py:391
  132.3 15.0 %all_to_all.15.got_ref = f32[32,16,128]{2,1,0:T(8,128)S(1)} all-to-all(f32[32,16,128]{2,1,0:T(8,128)S(1)} %bitcast.5), channel_id=1, replica_groups=mesh['row'=4,'col'=8] {'row','col'}, dimensions={0} | all-to-all | bytes 524288 | tf_op jit(solution)/shard_map/all_to_all | solution.py:403
  147.4 0.0 copy-done.3
  147.4 0.0 copy-done.4
  147.4 6.2 %shard_map.132 = f32[32,16,128]{2,1,0:T(8,128)S(1)} custom-call(f32[32,16,128]{2,1,0:T(8,128)S(1)} %all_to_all.15.got_ref, bf16[512,512]{1,0:T(8,128)(2,1)S(1)} %copy-done.3, bf16[512,512]{1,0:T(8,128)(2,1)S(1)} %copy-done.4, bf16[1024,1024]{1,0:T(8,128)(2,1)} %constant.16.clone.wh, bf16[1024,1024]{1,0:T(8,128)(2,1)} %constant.17.clone.wl), custom_call_target="tpu_custom_call" | custom-call | tf_op jit(solution)/shard_map/pallas_call | solution.py:410
  153.6 12.8 %all_to_all.16 = f32[32,16,128]{2,1,0:T(8,128)S(1)} all-to-all(f32[32,16,128]{2,1,0:T(8,128)S(1)} %shard_map.132), channel_id=1, replica_groups=mesh['row'=4,'col'=8] {'row','col'}, dimensions={0} | all-to-all | bytes 524288 | tf_op jit(solution)/shard_map/all_to_all | solution.py:437
  166.4 1.1 shard_map.133
  (1 shorter events, 0.0 us)
Async XLA Ops:
  0.6 123.8 %copy-start = (bf16[512,512]{1,0:T(8,128)(2,1)S(1)}, bf16[512,512]{1,0:T(8,128)(2,1)}, u32[]{:S(2)}) copy-start(bf16[512,512]{1,0:T(8,128)(2,1)} %constant.12.clone.high_ref) | copy-start | bytes 1572868
  0.6 123.8 %copy-start.1 = (bf16[512,512]{1,0:T(8,128)(2,1)S(1)}, bf16[512,512]{1,0:T(8,128)(2,1)}, u32[]{:S(2)}) copy-start(bf16[512,512]{1,0:T(8,128)(2,1)} %constant.13.clone.low_ref) | copy-start | bytes 1572868
  0.7 1.3 copy-start.2
  1.9 0.7 copy-start.5
  2.6 0.7 copy-start.7
  3.2 0.7 copy-start.8
  3.9 76.6 %copy-start.6 = (s32[2,3]{1,0:T(2,128)S(1)}, s32[2,3]{1,0:T(2,128)}, u32[]{:S(2)}) copy-start(s32[2,3]{1,0:T(2,128)} %corners_ref.1) | copy-start | bytes 76
  3.9 143.5 %copy-start.3 = (bf16[512,512]{1,0:T(8,128)(2,1)S(1)}, bf16[512,512]{1,0:T(8,128)(2,1)}, u32[]{:S(2)}) copy-start(bf16[512,512]{1,0:T(8,128)(2,1)} %constant.14.clone.vh) | copy-start | bytes 1572868
  3.9 143.5 %copy-start.4 = (bf16[512,512]{1,0:T(8,128)(2,1)S(1)}, bf16[512,512]{1,0:T(8,128)(2,1)}, u32[]{:S(2)}) copy-start(bf16[512,512]{1,0:T(8,128)(2,1)} %constant.15.clone.vl) | copy-start | bytes 1572868
  73.2 50.4 %all-to-all-start = ((f32[32,48,128]{2,1,0:T(8,128)}), f32[32,48,128]{2,1,0:T(8,128)S(1)}, u32[]{:S(2)}, u32[]{:S(2)}) async-start(f32[32,48,128]{2,1,0:T(8,128)} %get-tuple-element.8), calls=%async_computation | async-start | bytes 1572864 | tf_op jit(solution)/shard_map/all_to_all | solution.py:389
  123.6 0.9 copy-start.9

commit v2 on v1

--- a/solution.py
+++ b/solution.py
@@ -15,10 +15,12 @@
 SCREEN = 0.0025
 LANES = 128
 HALF = 64
+PLANES = 4
 GROUP = 8
 HIGHEST = lax.Precision.HIGHEST
 BF16 = jnp.bfloat16
 F32 = jnp.float32
+MESH = pl.DeviceIdType.MESH
 TILES = ((0, 0), (1, 0), (1, 1), (2, 1), (2, 2), (3, 2))
 
 
@@ -64,7 +66,6 @@
 
 def filter_kernel(
     reach,
-    mesh_sizes,
     own,
     corners_ref,
     signs_ref,
@@ -146,27 +147,30 @@
     coupling = jnp.where(lane % HALF < side, 1.0 / HALF_WIDTH, 0.0).astype(F32)
 
     def step(now, other, first, last):
-        def plane(y, total):
+        def planes(group, total):
+            top = group * PLANES + 1
             squares = None
-            before = now[y, pl.ds(0, orbs), :]
-            here = now[y, pl.ds(orbs, orbs), :]
+            before = [now[top + k, pl.ds(0, orbs), :] for k in range(PLANES)]
+            here = [now[top + k, pl.ds(orbs, orbs), :] for k in range(PLANES)]
             for x in range(side):
                 row = pl.ds(orbs * (x + 1), orbs)
-                after = now[y, pl.ds(orbs * (x + 2), orbs), :]
-                beside = (before + after) + (now[y - 1, row, :] + now[y + 1, row, :])
-                beside = beside + (
-                    pltpu.roll(here, 1, axis=1) + pltpu.roll(here, LANES - 1, axis=1)
-                )
-                result = coef[y - 1, pl.ds(x, 1), :] * here - coupling * beside
-                result = 0.5 * result if first else result - other[y, row, :]
-                other[y, row, :] = result
-                if last:
-                    square = result * result
-                    squares = square if squares is None else squares + square
+                after = [now[top + k, pl.ds(orbs * (x + 2), orbs), :] for k in range(PLANES)]
+                column = [now[top - 1, row, :]] + here + [now[top + PLANES, row, :]]
+                for k in range(PLANES):
+                    beside = (before[k] + after[k]) + (column[k] + column[k + 2])
+                    beside = beside + (
+                        pltpu.roll(here[k], 1, axis=1) + pltpu.roll(here[k], LANES - 1, axis=1)
+                    )
+                    result = coef[top + k - 1, pl.ds(x, 1), :] * here[k] - coupling * beside
+                    result = 0.5 * result if first else result - other[top + k, row, :]
+                    other[top + k, row, :] = result
+                    if last:
+                        square = result * result
+                        squares = square if squares is None else squares + square
                 before, here = here, after
             return total + squares if last else total
 
-        return lax.fori_loop(1, side + 1, plane, jnp.zeros((orbs, LANES), F32))
+        return lax.fori_loop(0, side // PLANES, planes, jnp.zeros((orbs, LANES), F32))
 
     step(even, odd, True, False)
     step(odd, even, False, False)
@@ -227,10 +231,11 @@
 
     cut = lane[:8]
 
+    start = jnp.full((8, LANES), corners_ref[0, 2], jnp.int32).astype(F32)
+
     def pack(i, carry):
         for j in range(reach[1]):
-            target = (row_index + i) % mesh_sizes[0] * mesh_sizes[1]
-            target = target + (col_index + j) % mesh_sizes[1]
+            slot = i * reach[1] + j
             for part in range(reach[2] // 8):
                 xs = pl.ds(pl.multiple_of(i * reach[2] + part * 8, 8), 8)
                 v = []
@@ -246,23 +251,48 @@
                     jnp.where(cut < 32, v[5], jnp.where(cut < 80, v[6], v[7])),
                 )
                 for t in range(3):
-                    send_ref[target, pl.ds((part * 3 + t) * 8, 8), :] = tiles[t]
+                    send_ref[slot, pl.ds((part * 3 + t) * 8, 8), :] = tiles[t]
+            send_ref[slot, pl.ds(reach[2] * 3, 8), :] = start
         return carry
 
     lax.fori_loop(0, reach[0], pack, 0)
 
 
-def gather_kernel(reach, mesh_sizes, own, side, starts_ref, got_ref, high_ref, low_ref, dens_ref, spec_ref, acc):
+def halo_kernel(reach, mesh_sizes, own, send_ref, got_ref, send_sems, recv_sems, local_sem):
     row_index, col_index = own()
+    rows, cols = mesh_sizes
+    barrier = pltpu.get_barrier_semaphore()
+    offsets = [(i, j) for i in range(reach[0]) for j in range(reach[1])][1:]
+    for i, j in offsets:
+        source = ((row_index + rows - i) % rows, (col_index + cols - j) % cols)
+        pl.semaphore_signal(barrier, inc=1, device_id=source, device_id_type=MESH)
+    pl.semaphore_wait(barrier, len(offsets))
+    copies = []
+    for i, j in offsets:
+        slot = i * reach[1] + j
+        copy = pltpu.make_async_remote_copy(
+            src_ref=send_ref.at[slot],
+            dst_ref=got_ref.at[slot],
+            send_sem=send_sems.at[slot],
+            recv_sem=recv_sems.at[slot],
+            device_id=((row_index + i) % rows, (col_index + j) % cols),
+            device_id_type=MESH,
+        )
+        copy.start()
+        copies.append(copy)
+    local = pltpu.make_async_copy(send_ref.at[0], got_ref.at[0], local_sem)
+    local.start()
+    local.wait()
+    for copy in copies:
+        copy.wait()
+
+
+def gather_kernel(reach, side, starts_ref, got_ref, high_ref, low_ref, dens_ref, spec_ref, acc):
     acc[...] = jnp.zeros_like(acc)
     depth = acc.shape[0]
     lane = lax.broadcasted_iota(jnp.int32, (8, LANES), 1)
 
-    def add(step, carry):
-        i = step // reach[1]
-        j = step % reach[1]
-        source = (row_index + mesh_sizes[0] - i) % mesh_sizes[0] * mesh_sizes[1]
-        source = source + (col_index + mesh_sizes[1] - j) % mesh_sizes[1]
+    def add(source, carry):
         start = starts_ref[source]
         tile = start // LANES
         inner = start % LANES
@@ -287,8 +317,50 @@
     spec_ref[...] = dot3((high_ref[...], low_ref[...]), split2(whole), ((1,), (1,)))
 
 
-def screen_kernel(rows, cols, own, sizes, got_ref, vh, vl, wh, wl, out_ref):
+def screen_kernel(
+    rows, cols, own, sizes, spec_ref, vh, vl, wh, wl, zh, zl, hart_ref, got_ref, out_ref, back_ref,
+    send_sems, recv_sems,
+):
     row_index, col_index = own()
+    me = row_index * cols + col_index
+    peers = rows * cols
+    barrier = pltpu.get_barrier_semaphore()
+
+    def device(offset):
+        other = (me + offset) % peers
+        return other, (other // cols, other % cols)
+
+    def greet(offset, carry):
+        pl.semaphore_signal(barrier, inc=1, device_id=device(offset)[1], device_id_type=MESH)
+        return carry
+
+    def exchange(source_ref, target_ref, phase):
+        def copy(offset):
+            other, where = device(offset)
+            return pltpu.make_async_remote_copy(
+                src_ref=source_ref.at[other],
+                dst_ref=target_ref.at[me],
+                send_sem=send_sems.at[phase, offset],
+                recv_sem=recv_sems.at[phase, offset],
+                device_id=where,
+                device_id_type=MESH,
+            )
+
+        def start(offset, carry):
+            copy(offset).start()
+            return carry
+
+        def finish(offset, carry):
+            copy(offset).wait()
+            return carry
+
+        lax.fori_loop(1, peers, start, 0)
+        target_ref[me] = source_ref[me]
+        lax.fori_loop(1, peers, finish, 0)
+
+    lax.fori_loop(1, peers, greet, 0)
+    pl.semaphore_wait(barrier, peers - 1)
+    exchange(spec_ref, got_ref, 0)
     thin = got_ref.shape[1]
     nx, ny, nz = sizes
     cx, cy = nx // rows, ny // cols
@@ -343,11 +415,18 @@
     for r in range(rows):
         for c in range(cols):
             out_ref[r * cols + c] = by_x[c * thin : (c + 1) * thin, r * LANES : (r + 1) * LANES]
+    exchange(out_ref, back_ref, 1)
+    back = back_ref[...].reshape(peers * thin, LANES)
+    to_cells(back, zh, zl, hart_ref)
+
+
+def to_cells(spec, high_ref, low_ref, out_ref):
+    spec = jnp.transpose(spec, (1, 0))
+    out_ref[...] = dot3(split2(spec), (high_ref[...], low_ref[...])).reshape(out_ref.shape)
 
 
 def back_kernel(got_ref, high_ref, low_ref, out_ref):
-    spec = jnp.transpose(got_ref[...], (1, 0))
-    out_ref[...] = dot3(split2(spec), (high_ref[...], low_ref[...])).reshape(out_ref.shape)
+    to_cells(got_ref[...], high_ref, low_ref, out_ref)
 
 
 def shards(orbitals, potential_boxes, corners, signs, counts, *, rows, cols, out_block):
@@ -365,13 +444,13 @@
     vmem = pl.BlockSpec(memory_space=pltpu.VMEM)
     smem = pl.BlockSpec(memory_space=pltpu.SMEM)
     params = pltpu.CompilerParams(vmem_limit_bytes=52 * 2**20)
-    starts = lax.all_gather(corners[0, 2], ("row", "col"))
-    block_rows = cx // 8 * 3 * 8
+    slots = reach[0] * reach[1]
+    block = jax.ShapeDtypeStruct((slots, cx * 3 + 8, LANES), F32)
     filtered, send = pl.pallas_call(
-        functools.partial(filter_kernel, reach, mesh_sizes, own),
+        functools.partial(filter_kernel, reach, own),
         out_shape=(
             jax.ShapeDtypeStruct(orbitals.shape, BF16),
-            jax.ShapeDtypeStruct((peers, block_rows, LANES), F32),
+            block,
         ),
         in_specs=[smem] * 3 + [vmem] * 2,
         out_specs=(vmem, vmem),
@@ -386,10 +465,22 @@
         ],
         compiler_params=params,
     )(corners, signs, counts, orbitals, potential_boxes)
-    got = lax.all_to_all(send, ("row", "col"), 0, 0, tiled=True)
+    got = pl.pallas_call(
+        functools.partial(halo_kernel, reach, mesh_sizes, own),
+        out_shape=block,
+        in_specs=[vmem],
+        out_specs=vmem,
+        scratch_shapes=[
+            pltpu.SemaphoreType.DMA((slots,)),
+            pltpu.SemaphoreType.DMA((slots,)),
+            pltpu.SemaphoreType.DMA,
+        ],
+        compiler_params=pltpu.CompilerParams(collective_id=0, has_side_effects=True),
+    )(send)
+    starts = got[:, cx * 3, 0].astype(jnp.int32)
     z_high, z_low = split_table(real_basis(nz))
     density, spec = pl.pallas_call(
-        functools.partial(gather_kernel, reach, mesh_sizes, own, side),
+        functools.partial(gather_kernel, reach, side),
         out_shape=(
             jax.ShapeDtypeStruct(out_block, F32),
             jax.ShapeDtypeStruct((nz, cx * cy), F32),
@@ -400,20 +491,29 @@
         compiler_params=params,
     )(starts, got, z_high, z_low)
     spec = spec.reshape(peers, thin, cx * cy)
-    spec = lax.all_to_all(spec, ("row", "col"), 0, 0, tiled=True)
     x_basis, y_basis = real_basis(nx), real_basis(ny)
     if thin % 8 == 0 and ny * cx <= 1024:
         x_table = np.kron(x_basis.T, np.eye(cy))
         y_table = np.einsum("mcy,xw->cxymw", y_basis.reshape(ny, cols, cy), np.eye(cx))
         y_table = y_table.reshape(cols * cx * cy, cols, cy, cx).transpose(0, 1, 3, 2)
         y_table = y_table.reshape(cols * cx * cy, cols * cx * cy)
-        spec = pl.pallas_call(
+        blocks = pltpu.VMEM(spec.shape, F32)
+        hartree = pl.pallas_call(
             functools.partial(screen_kernel, rows, cols, own, (nx, ny, nz)),
-            out_shape=jax.ShapeDtypeStruct(spec.shape, F32),
-            in_specs=[vmem] * 5,
+            out_shape=jax.ShapeDtypeStruct(out_block, F32),
+            in_specs=[vmem] * 7,
             out_specs=vmem,
-            compiler_params=params,
-        )(spec, *split_table(x_table), *split_table(y_table))
+            scratch_shapes=[
+                blocks,
+                blocks,
+                blocks,
+                pltpu.SemaphoreType.DMA((2, peers)),
+                pltpu.SemaphoreType.DMA((2, peers)),
+            ],
+            compiler_params=pltpu.CompilerParams(
+                collective_id=1, has_side_effects=True, vmem_limit_bytes=52 * 2**20
+            ),
+        )(spec, *split_table(x_table), *split_table(y_table), z_high, z_low)
     else:
         x_basis, y_basis = x_basis.astype(np.float32), y_basis.astype(np.float32)
 
@@ -424,6 +524,7 @@
             return wave * wave
 
         r, c = own()
+        spec = lax.all_to_all(spec, ("row", "col"), 0, 0, tiled=True)
         grid = spec.reshape(rows, cols, thin, cx, cy).transpose(2, 0, 3, 1, 4)
         grid = grid.reshape(thin, nx, ny)
         grid = jnp.einsum("kxy,ax,by->kab", grid, x_basis, y_basis, precision=HIGHEST)
@@ -433,15 +534,14 @@
         grid = grid * jnp.where(k_square > 0, SCREEN / (k_square + SCREEN), 0.0)
         grid = jnp.einsum("kab,ax,by->kxy", grid, x_basis, y_basis, precision=HIGHEST)
         grid = grid.reshape(thin, rows, cx, cols, cy).transpose(1, 3, 0, 2, 4)
-        spec = grid.reshape(spec.shape)
-    spec = lax.all_to_all(spec, ("row", "col"), 0, 0, tiled=True).reshape(nz, cx * cy)
-    hartree = pl.pallas_call(
-        back_kernel,
-        out_shape=jax.ShapeDtypeStruct(out_block, F32),
-        in_specs=[vmem] * 3,
-        out_specs=vmem,
-        compiler_params=params,
-    )(spec, z_high, z_low)
+        spec = lax.all_to_all(grid.reshape(spec.shape), ("row", "col"), 0, 0, tiled=True)
+        hartree = pl.pallas_call(
+            back_kernel,
+            out_shape=jax.ShapeDtypeStruct(out_block, F32),
+            in_specs=[vmem] * 3,
+            out_specs=vmem,
+            compiler_params=params,
+        )(spec.reshape(nz, cx * cy), z_high, z_low)
     return (filtered, density, hartree)
 
 

time: 168 us -> 120 us (0.71)
  blocking collectives: 69.6 us -> 0 us
  Pallas kernels: 84.5 us -> 113 us
  starting transfers between devices: 7.3 us -> 0 us
    all_gather x1 -> x0, blocking collectives: 41.8 us -> none  [shards(): starts = lax.all_gather(corners[0, 2], ('row', 'col'))]
    all_to_all x2 -> x0, blocking collectives: 27.8 us -> none  [the longest x1 15 us: shards(): spec = lax.all_to_all(spec, ('row', 'col'), 0, 0, tiled=True)]
    pallas_call x1, Pallas kernels: 6.17 us -> 27.7 us  [shards(): pl.pallas_call(functools.partial(screen_kernel, rows, cols, own, (nx, ny,...]
    all_to_all x1 -> x0, starting transfers between devices: 7.3 us -> none  [shards(): got = lax.all_to_all(send, ('row', 'col'), 0, 0, tiled=True)]
    pallas_call x3, Pallas kernels: 78.3 us -> 85.3 us  [the longest x1 49 us: shards(): pl.pallas_call(functools.partial(filter_kernel, reach, own), out_shape=(j...]
    unnamed x22 -> x19, local copies, waits for them, and re-layouts: 4.82 us -> 4.85 us
  transfers between devices with their start and end apart: 1 -> 0, of which waited for: 0 -> 0; matrix products, arithmetic and copies ran while one was open for 1% -> 0% of each run, Pallas kernels for 0% -> 0%
where the time goes in v2:
time: 120 us
  Pallas kernels  113 us (94%)
  local copies, waits for them, and re-layouts  4.85 us (4%)
  other arithmetic  1.49 us (1%)
    pallas_call x1, Pallas kernels, shards(): pl.pallas_call(functools.partial(filter_kernel, reach, own), out_shape=(j...  49 us
    pallas_call x1, Pallas kernels, shards(): pl.pallas_call(functools.partial(halo_kernel, reach, mesh_sizes, own), ou...  28.8 us
    pallas_call x1, Pallas kernels, shards(): pl.pallas_call(functools.partial(screen_kernel, rows, cols, own, (nx, ny,...  27.7 us
    pallas_call x1, Pallas kernels, shards(): pl.pallas_call(functools.partial(gather_kernel, reach, side), out_shape=(...  7.45 us
    unnamed x19, local copies, waits for them, and re-layouts  4.85 us

profile of v2, /device:TPU:0, one launch (start us, length us, event | category | flops | bytes accessed | tf_op | source)
XLA Modules:
  0.0 120.0 jit_solution(15104534982309439335)
XLA Ops:
  0.6 0.0 copy-start
  0.6 0.0 copy-start.1
  0.7 0.0 copy-start.2
  0.7 1.2 %copy-done.2 = f32[2,48,2304]{2,1,0:T(8,128)S(1)} copy-done((f32[2,48,2304]{2,1,0:T(8,128)S(1)}, f32[2,48,2304]{2,1,0:T(8,128)}, u32[]{:S(2)}) %copy-start.2) | copy-done | bytes 884760
  1.9 0.0 copy-start.6
  1.9 0.7 copy-done.6
  2.6 0.0 copy-start.7
  2.6 0.7 copy-done.7
  3.2 0.0 copy-start.8
  3.2 0.7 copy-done.8
  3.9 0.0 copy-start.4
  3.9 0.0 copy-start.5
  3.9 49.0 %shard_map.130 = (bf16[2,8,48,2304]{3,2,1,0:T(8,128)(2,1)}, f32[28,56,128]{2,1,0:T(8,128)S(1)}) custom-call(s32[2,3]{1,0:T(2,128)S(1)} %copy-done.6, s32[2]{0:T(128)S(1)} %copy-done.7, s32[2]{0:T(128)S(1)} %copy-done.8, bf16[2,8,48,2304]{3,2,1,0:T(8,128)(2,1)} %orb_ref.1, f32[2,48,2304]{2,1,0:T(8,128)S(1)} %copy-done.2), custom_call_target="tpu_custom_call" | custom-call | tf_op jit(solution)/shard_map/pallas_call | solution.py:449
  53.0 0.0 copy-start.3
  53.0 0.9 copy-done.3
  53.8 28.8 %shard_map.131.got_ref = f32[28,56,128]{2,1,0:T(8,128)} custom-call(f32[28,56,128]{2,1,0:T(8,128)} %copy-done.3), custom_call_target="tpu_custom_call" | custom-call | tf_op jit(solution)/shard_map/pallas_call | solution.py:468
  82.6 1.5 %convert_reduce_fusion.starts_ref = s32[28]{0:T(128)S(1)} fusion(f32[28,56,128]{2,1,0:T(8,128)} %shard_map.131.got_ref), kind=kLoop, calls=%fused_computation | loop fusion | flops 28 | bytes 224 | tf_op jit(solution)/shard_map/convert_element_type | solution.py:480
  84.1 0.0 copy-done
  84.1 0.0 copy-done.1
  84.2 7.5 %shard_map.132 = (f32[16,8,512]{2,1,0:T(8,128)}, f32[512,128]{1,0:T(8,128)S(1)}) custom-call(s32[28]{0:T(128)S(1)} %convert_reduce_fusion.starts_ref, f32[28,56,128]{2,1,0:T(8,128)} %shard_map.131.got_ref, bf16[512,512]{1,0:T(8,128)(2,1)S(1)} %copy-done.1, bf16[512,512]{1,0:T(8,128)(2,1)S(1)} %copy-done), custom_call_target="tpu_custom_call" | custom-call | tf_op jit(solution)/shard_map/pallas_call | solution.py:482
  91.6 0.0 copy-done.4
  91.6 0.0 copy-done.5
  91.6 27.7 %shard_map.133 = f32[16,8,512]{2,1,0:T(8,128)S(1)} custom-call(f32[32,16,128]{2,1,0:T(8,128)S(1)} %bitcast.1, bf16[512,512]{1,0:T(8,128)(2,1)S(1)} %copy-done.5, bf16[512,512]{1,0:T(8,128)(2,1)S(1)} %copy-done.4, bf16[1024,1024]{1,0:T(8,128)(2,1)} %constant.16.clone.wh, bf16[1024,1024]{1,0:T(8,128)(2,1)} %constant.17.clone.wl, ...), custom_call_target="tpu_custom_call" | custom-call | tf_op jit(solution)/shard_map/pallas_call | solution.py:501
  119.3 0.7 copy.15
Async XLA Ops:
  0.6 83.5 %copy-start = (bf16[512,512]{1,0:T(8,128)(2,1)S(1)}, bf16[512,512]{1,0:T(8,128)(2,1)}, u32[]{:S(2)}) copy-start(bf16[512,512]{1,0:T(8,128)(2,1)} %constant.13.clone.low_ref.zl) | copy-start | bytes 1572868
  0.6 83.5 %copy-start.1 = (bf16[512,512]{1,0:T(8,128)(2,1)S(1)}, bf16[512,512]{1,0:T(8,128)(2,1)}, u32[]{:S(2)}) copy-start(bf16[512,512]{1,0:T(8,128)(2,1)} %constant.12.clone.high_ref.zh) | copy-start | bytes 1572868
  0.7 1.3 %copy-start.2 = (f32[2,48,2304]{2,1,0:T(8,128)S(1)}, f32[2,48,2304]{2,1,0:T(8,128)}, u32[]{:S(2)}) copy-start(f32[2,48,2304]{2,1,0:T(8,128)} %pot_ref.1) | copy-start | bytes 2654212
  1.9 0.7 copy-start.6
  2.6 0.7 copy-start.7
  3.2 0.7 copy-start.8
  3.9 87.7 %copy-start.4 = (bf16[512,512]{1,0:T(8,128)(2,1)S(1)}, bf16[512,512]{1,0:T(8,128)(2,1)}, u32[]{:S(2)}) copy-start(bf16[512,512]{1,0:T(8,128)(2,1)} %constant.15.clone.vl) | copy-start | bytes 1572868
  3.9 87.7 %copy-start.5 = (bf16[512,512]{1,0:T(8,128)(2,1)S(1)}, bf16[512,512]{1,0:T(8,128)(2,1)}, u32[]{:S(2)}) copy-start(bf16[512,512]{1,0:T(8,128)(2,1)} %constant.14.clone.vh) | copy-start | bytes 1572868
  53.0 0.9 copy-start.3
